TPU v7x, 256 devices: a whole 4x4x8 slice. The times are simulated.
256 devices in a mesh: tile: 32 (over y, x, core), cls: 8 (over z).
Axes of the slice: x: 4, y: 4, z: 8, core: 2. Of those that a mesh axis runs over, the one named last changes fastest.
Arguments:
- subvols: bfloat16 [8192, 32768], P(('tile', 'cls')), may hold values from -16 to 16
- tomogram: int32 [8192, 1], P(('tile', 'cls')), may hold values from 0 to 31; in each aligned block of 32 rows (0 to 31, 32 to 63, ...) at most 2 rows name the same one
- sharpness: bfloat16 [8192], P(('tile', 'cls')), may hold values from 0.5 to 6
- references: bfloat16 [8, 32768], P('cls'), may hold values from -6 to 6
- interp: bfloat16 [4, 3, 32, 32], replicated, may hold values from -0.4 to 1.1
- weighting: bfloat16 [32, 4, 32768], P('tile'), may hold values from 0.099609375 to 1
Outputs:
- updated: bfloat16 [8, 32768], P('cls')
- posterior: float32 [8192, 8], P(('tile', 'cls'))
Inputs may be any that keep to these rules, and one draw needn't show every extreme that they name: In the rows of one device no tomogram appears more than 2 times, and some tomogram exactly that many times.
All inputs are finite; a program needn't handle non-finite values.
Results may differ from a plain program's by a relative error of at most 0.03.
Values may be sent and summed in bfloat16 or wider, within the bound.
A program may use at most 128 MiB of HBM per device.

v0:
```python
import math

import jax
import jax.numpy as jnp
from jax import lax
from jax.sharding import PartitionSpec as P


def rotate(volumes, interp):
    edge = interp.shape[-1]
    count = volumes.shape[0]
    volume = volumes.reshape(count, edge, edge, edge)
    first_pass = jnp.einsum(
        "rijl,ocl->orcij", volume, interp[:, 2], preferred_element_type=jnp.float32
    ).astype(jnp.bfloat16)
    second_pass = jnp.einsum(
        "orcij,obj->orbci", first_pass, interp[:, 1], preferred_element_type=jnp.float32
    ).astype(jnp.bfloat16)
    third_pass = jnp.einsum(
        "orbci,oai->orabc", second_pass, interp[:, 0], preferred_element_type=jnp.float32
    ).astype(jnp.bfloat16)
    return third_pass.reshape(interp.shape[0], count, edge**3)


def unrotate(volumes, interp):
    edge = interp.shape[-1]
    orients, count = (volumes.shape[0], volumes.shape[1])
    volume = volumes.reshape(orients, count, edge, edge, edge)
    back_one = jnp.einsum(
        "orabc,ocl->orlab", volume, interp[:, 2], preferred_element_type=jnp.float32
    ).astype(jnp.bfloat16)
    back_two = jnp.einsum(
        "orlab,obj->orjla", back_one, interp[:, 1], preferred_element_type=jnp.float32
    ).astype(jnp.bfloat16)
    back_three = jnp.einsum(
        "orjla,oai->orijl", back_two, interp[:, 0], preferred_element_type=jnp.float32
    ).astype(jnp.bfloat16)
    return back_three.reshape(orients, count, edge**3)


def normalize(summed):
    spread = jnp.sqrt(jnp.mean(summed * summed, axis=1, keepdims=True) + 1e-06)
    return (summed / spread).astype(jnp.bfloat16)


def shards(subvols, tomogram, sharpness, references, interp, weighting):
    sub_count, voxels = subvols.shape
    tile_count = lax.axis_size("tile")
    capacity = 2 * sub_count // tile_count
    target = tomogram[:, 0]
    onehot = (target[:, None] == jnp.arange(tile_count, dtype=jnp.int32)[None, :]).astype(jnp.int32)
    within = jnp.sum((jnp.cumsum(onehot, axis=0) - onehot) * onehot, axis=1)
    position = target * capacity + within
    outgoing = jnp.zeros((tile_count * capacity, voxels), jnp.bfloat16).at[position].set(subvols)
    sharp_out = jnp.zeros((tile_count * capacity,), jnp.bfloat16).at[position].set(sharpness)
    received, sharp_in = (
        lax.all_to_all(outgoing, "tile", split_axis=0, concat_axis=0, tiled=True),
        lax.all_to_all(sharp_out, "tile", split_axis=0, concat_axis=0, tiled=True),
    )
    orients = interp.shape[0]
    tomo_weight = weighting[0].astype(jnp.float32)[:, None, :]
    scale = sharp_in.astype(jnp.float32)[:, None] / math.sqrt(voxels)
    own_refs = references
    all_refs = None
    posterior = None
    all_refs = lax.all_gather(own_refs, "cls", axis=0, tiled=True)
    rotated = rotate(all_refs, interp)
    ref_count = rotated.shape[1]
    filtered = (
        (tomo_weight * rotated.astype(jnp.float32))
        .astype(jnp.bfloat16)
        .reshape(orients * ref_count, voxels)
    )
    scores = (
        lax.dot_general(
            received, filtered, (((1,), (1,)), ((), ())), preferred_element_type=jnp.float32
        )
        * scale
    )
    weights = jax.nn.softmax(scores, axis=1)
    weights_q = weights.astype(jnp.bfloat16)
    accum = lax.dot_general(
        weights_q, received, (((0,), (0,)), ((), ())), preferred_element_type=jnp.float32
    )
    accum = (accum.reshape(orients, ref_count, voxels) * tomo_weight).astype(jnp.bfloat16)
    partial_value = jnp.sum(unrotate(accum, interp).astype(jnp.float32), axis=0)
    class_prob = jnp.sum(weights.reshape(-1, orients, ref_count), axis=1)
    returned = lax.all_to_all(class_prob, "tile", split_axis=0, concat_axis=0, tiled=True)
    posterior = returned[position]
    tile_sums = lax.psum(partial_value.astype(jnp.bfloat16), "tile")
    own_sums = lax.psum_scatter(tile_sums, "cls", scatter_dimension=0, tiled=True).astype(
        jnp.float32
    )
    own_refs = normalize(own_sums)
    return (own_refs, posterior)


def solution(mesh):
    in_specs = (
        P(("tile", "cls"), None),
        P(("tile", "cls"), None),
        P(("tile", "cls")),
        P("cls", None),
        P(),
        P("tile", None, None),
    )
    out_specs = (P("cls", None), P(("tile", "cls"), None))
    return jax.shard_map(shards, mesh=mesh, in_specs=in_specs, out_specs=out_specs, check_vma=False)
```

profile of v0, /device:TPU:1, one launch (start us, length us, event | category | flops | bytes accessed | tf_op | source)
XLA Modules:
  0.0 473.7 jit_solution(17160844840589937369)
XLA Ops:
  11.1 8.6 %all-to-all-start.1 = ((bf16[32,2,1]{1,2,0:T(2,128)(2,1)}), bf16[32,2,1]{1,2,0:T(2,128)(2,1)S(1)}, u32[]{:S(2)}, u32[]{:S(2)}) async-start(bf16[32,2,1]{1,2,0:T(2,128)(2,1)} %all_to_all.30), calls=%async_computation.1 | async-start | bytes 32768 | tf_op jit(solution)/shard_map/all_to_all | solution.py:58
  19.7 6.9 %scatter_custom_fusion = bf16[64,32768]{1,0:T(8,128)(2,1)} fusion(s32[32]{0:T(128)S(1)} %fusion.41, bf16[32,32768]{1,0:T(8,128)(2,1)} %param.6, bf16[]{:T(256)} %constant.9.clone.1), kind=kCustom, calls=%fused_computation.20 | custom fusion | bytes 4194816 | tf_op jit(solution)/shard_map/scatter | solution.py:54
  26.6 7.7 %all_to_all.22 = bf16[32,2,32768]{2,1,0:T(2,128)(2,1)} reshape(bf16[64,32768]{1,0:T(8,128)(2,1)} %scatter_custom_fusion) | data formatting | bytes 8388608 | tf_op jit(solution)/shard_map/all_to_all | solution.py:57
  34.3 25.5 %all-gather = bf16[8,1,32768]{2,1,0:T(2,128)(2,1)S(1)} all-gather(bf16[1,1,32768]{2,1,0:T(2,128)(2,1)S(1)} %bitcast.88), channel_id=1, replica_groups=mesh['tile'=32,'cls'=8] {'cls'}, dimensions={0}, use_global_device_ids=true | all-gather | bytes 589824 | tf_op jit(solution)/shard_map/all_gather | solution.py:66
  64.6 6.6 %convert_bitcast_fusion.3 = bf16[4,8,32,32,32]{4,2,3,1,0:T(8,128)(2,1)} fusion(bf16[8,32,32,32,1]{3,2,1,0,4:T(8,128)(2,1)S(1)} %reshape.106, bf16[4,3,32,32]{3,2,1,0:T(8,128)(2,1)S(1)} %copy-done), kind=kOutput, calls=%fused_computation.14 | convolution fusion | flops 68157440 | bytes 4227072 | tf_op jit(solution)/shard_map/rijl,ocl->orcij/dot_general | solution.py:13
  71.2 10.1 %convert_bitcast_fusion.2 = bf16[4,8,32,32,32]{2,4,3,1,0:T(8,128)(2,1)} fusion(bf16[4,8,32,32,32]{4,2,3,1,0:T(8,128)(2,1)} %convert_bitcast_fusion.3, bf16[4,3,32,32]{3,2,1,0:T(8,128)(2,1)S(1)} %copy-done), kind=kOutput, calls=%fused_computation.13 | convolution fusion | flops 68157440 | bytes 4227072 | tf_op jit(solution)/shard_map/orcij,obj->orbci/dot_general | solution.py:16
  81.2 16.8 %copy.28 = bf16[4,8,32,32,32]{4,3,2,1,0:T(8,128)(2,1)} copy(bf16[4,8,32,32,32]{2,4,3,1,0:T(8,128)(2,1)} %convert_bitcast_fusion.2) | data formatting | bytes 4194304 | tf_op jit(solution)/shard_map/convert_element_type | solution.py:18
  98.1 11.4 %convert_bitcast_fusion = f32[4,8,32,32,32]{2,4,3,1,0:T(8,128)} fusion(bf16[4,8,32,32,32]{4,3,2,1,0:T(8,128)(2,1)} %copy.28, bf16[4,3,32,32]{3,2,1,0:T(8,128)(2,1)S(1)} %copy-done), kind=kOutput, calls=%fused_computation.5 | convolution fusion | flops 69206016 | bytes 6324224 | tf_op jit(solution)/shard_map/orbci,oai->orabc/dot_general | solution.py:19
  109.5 19.9 %copy.29 = f32[4,8,32,32,32]{4,3,2,1,0:T(8,128)} copy(f32[4,8,32,32,32]{2,4,3,1,0:T(8,128)} %convert_bitcast_fusion) | data formatting | bytes 8388608 | tf_op jit(solution)/shard_map/convert_element_type | solution.py:70
  129.4 11.6 %reshape.77 = f32[4,8,32768]{2,1,0:T(8,128)} reshape(f32[4,8,32,32,32]{4,3,2,1,0:T(8,128)} %copy.29) | data formatting | bytes 8388608 | tf_op jit(solution)/shard_map/convert_element_type | solution.py:70
  141.0 12.9 %all-to-all-start = ((bf16[32,2,32768]{2,1,0:T(2,128)(2,1)}), bf16[32,2,32768]{2,1,0:T(2,128)(2,1)}, u32[]{:S(2)}, u32[]{:S(2)}) async-start(bf16[32,2,32768]{2,1,0:T(2,128)(2,1)} %all_to_all.22), calls=%async_computation | async-start | bytes 8388608 | tf_op jit(solution)/shard_map/all_to_all | solution.py:57
  154.2 50.0 %all-to-all-done = bf16[32,2,32768]{2,1,0:T(2,128)(2,1)} async-done(((bf16[32,2,32768]{2,1,0:T(2,128)(2,1)}), bf16[32,2,32768]{2,1,0:T(2,128)(2,1)}, u32[]{:S(2)}, u32[]{:S(2)}) %all-to-all-start) | async-done | bytes 4194336 | tf_op jit(solution)/shard_map/all_to_all | solution.py:57
  204.2 7.4 %all_to_all.24 = bf16[64,32768]{1,0:T(8,128)(2,1)} reshape(bf16[32,2,32768]{2,1,0:T(2,128)(2,1)} %all-to-all-done) | data formatting | bytes 8388608 | tf_op jit(solution)/shard_map/all_to_all | solution.py:57
  211.6 4.7 fusion.44
  216.3 7.2 %reshape.109 = bf16[64,32768,1]{1,0,2:T(8,128)(2,1)} reshape(bf16[32,2,32768]{2,1,0:T(2,128)(2,1)} %all-to-all-done) | data formatting | bytes 8388608 | tf_op jit(solution)/shard_map/all_to_all | solution.py:57
  226.5 7.9 %reshape.74 = bf16[4,8,32,32,32]{4,3,2,1,0:T(8,128)(2,1)} reshape(bf16[4,8,32768]{2,1,0:T(8,128)(2,1)S(1)} %fusion) | data formatting | bytes 4194304 | tf_op jit(solution)/shard_map/reshape | solution.py:28
  234.5 9.7 %convert_bitcast_fusion.1 = bf16[4,8,32,32,32]{2,3,4,1,0:T(8,128)(2,1)} fusion(bf16[4,8,32,32,32]{4,3,2,1,0:T(8,128)(2,1)} %reshape.74, bf16[4,3,32,32]{3,2,1,0:T(8,128)(2,1)S(1)} %copy-done), kind=kOutput, calls=%fused_computation.11 | convolution fusion | flops 136314880 | bytes 4259840 | tf_op jit(solution)/shard_map/orlab,obj->orjla/dot_general | solution.py:32
  244.1 19.8 %copy.32 = bf16[4,8,32,32,32]{4,3,2,1,0:T(8,128)(2,1)} copy(bf16[4,8,32,32,32]{2,3,4,1,0:T(8,128)(2,1)} %convert_bitcast_fusion.1) | data formatting | bytes 4194304 | tf_op jit(solution)/shard_map/convert_element_type | solution.py:34
  263.9 5.9 %convert_reduce_fusion = bf16[8,32,32,32]{3,2,1,0:T(8,128)(2,1)S(1)} fusion(bf16[4,8,32,32,32]{4,3,2,1,0:T(8,128)(2,1)} %copy.32, bf16[4,3,32,32]{3,2,1,0:T(8,128)(2,1)S(1)} %copy-done), kind=kOutput, calls=%fused_computation.10 | convolution fusion | flops 68943872 | bytes 2654208 | tf_op jit(solution)/shard_map/orjla,oai->orijl/dot_general | solution.py:35
  269.8 4.6 copy.33
  274.5 4.6 reduce_sum.59
  280.4 7.0 %all-to-all-start.2 = ((f32[32,2,8]{2,1,0:T(2,128)}), f32[32,2,8]{2,1,0:T(2,128)S(1)}, u32[]{:S(2)}, u32[]{:S(2)}) async-start(f32[32,2,8]{2,1,0:T(2,128)} %bitcast.24), calls=%async_computation.2 | async-start | bytes 65536 | tf_op jit(solution)/shard_map/all_to_all | solution.py:88
  287.5 58.0 %all-reduce.6.cloned.1.call-done = bf16[8,32768]{1,0:T(8,128)(2,1)} async-done(((bf16[8,32768]{1,0:T(8,128)(2,1)}), bf16[8,32768]{1,0:T(8,128)(2,1)}) %all-reduce.6.cloned.1.call-update) | async-done | bytes 524304
  349.3 113.2 %all-reduce.4.cloned.1.call-done = bf16[1,32768]{1,0:T(2,128)(2,1)} async-done(((bf16[1,32768]{1,0:T(2,128)(2,1)}), bf16[1,32768]{1,0:T(2,128)(2,1)}) %all-reduce.4.cloned.1.call-update) | async-done | bytes 65552 | tf_op jit(solution)/shard_map/psum | solution.py:90
  (36 shorter events, 20.5 us)
Async XLA Ops:
  11.1 129.9 %all-to-all-start.1 = ((bf16[32,2,1]{1,2,0:T(2,128)(2,1)}), bf16[32,2,1]{1,2,0:T(2,128)(2,1)S(1)}, u32[]{:S(2)}, u32[]{:S(2)}) async-start(bf16[32,2,1]{1,2,0:T(2,128)(2,1)} %all_to_all.30), calls=%async_computation.1 | async-start | bytes 32768 | tf_op jit(solution)/shard_map/all_to_all | solution.py:58
  26.6 7.7 %copy-start.2 = (bf16[1,32768]{1,0:T(2,128)(2,1)S(1)}, bf16[1,32768]{1,0:T(2,128)(2,1)}, u32[]{:S(2)}) copy-start(bf16[1,32768]{1,0:T(2,128)(2,1)} %param.9) | copy-start | bytes 196612
  34.3 30.3 %copy-start = (bf16[4,3,32,32]{3,2,1,0:T(8,128)(2,1)S(1)}, bf16[4,3,32,32]{3,2,1,0:T(8,128)(2,1)}, u32[]{:S(2)}) copy-start(bf16[4,3,32,32]{3,2,1,0:T(8,128)(2,1)} %param.10) | copy-start | bytes 73732
  141.0 13.0 %copy-start.1 = (bf16[1,4,32768]{2,1,0:T(4,128)(2,1)S(1)}, bf16[1,4,32768]{2,1,0:T(4,128)(2,1)}, u32[]{:S(2)}) copy-start(bf16[1,4,32768]{2,1,0:T(4,128)(2,1)} %param.11) | copy-start | bytes 786436
  141.0 63.2 %all-to-all-start = ((bf16[32,2,32768]{2,1,0:T(2,128)(2,1)}), bf16[32,2,32768]{2,1,0:T(2,128)(2,1)}, u32[]{:S(2)}, u32[]{:S(2)}) async-start(bf16[32,2,32768]{2,1,0:T(2,128)(2,1)} %all_to_all.22), calls=%async_computation | async-start | bytes 8388608 | tf_op jit(solution)/shard_map/all_to_all | solution.py:57
  153.9 191.6 %all-reduce.6.cloned.1.call-start = ((), (), s32[]{:S(2)}) async-start(), calls=%async_computation.4 | async-start | bytes 1048576
  269.8 9.3 %copy-start.3 = (u32[256]{0:T(256)S(1)}, u32[256]{0:T(256)}, u32[]{:S(2)}) copy-start(u32[256]{0:T(256)} %constant.37) | copy-start | bytes 3076
  280.4 67.6 %all-to-all-start.2 = ((f32[32,2,8]{2,1,0:T(2,128)}), f32[32,2,8]{2,1,0:T(2,128)S(1)}, u32[]{:S(2)}, u32[]{:S(2)}) async-start(f32[32,2,8]{2,1,0:T(2,128)} %bitcast.24), calls=%async_computation.2 | async-start | bytes 65536 | tf_op jit(solution)/shard_map/all_to_all | solution.py:88
  287.5 175.0 %all-reduce.4.cloned.1.call-start = ((), (), s32[]{:S(2)}) async-start(), calls=%async_computation.3 | async-start | bytes 262144 | tf_op jit(solution)/shard_map/psum | solution.py:90
Sparse Core Ops, SparseCore 0:
  279.2 66.2 all-reduce.5
  349.6 112.7 all-reduce.3
where the time goes:
time: 480 us; the launch traced here: 474 us
  waiting for transfers between devices  221 us (46%)
  local copies, waits for them, and re-layouts  123 us (26%)
  matrix products  51.2 us (11%)
  starting transfers between devices  28.6 us (6%)
  blocking collectives  25.5 us (5%)
  between operations  15.1 us (3%)
  other arithmetic  9.09 us (2%)
    psum x1, waiting for transfers between devices, shards(): tile_sums = lax.psum(partial_value.astype(jnp.bfloat16), 'tile')  113 us
    unnamed x3, waiting for transfers between devices  58.1 us
    all_to_all x1, waiting for transfers between devices, shards(): lax.all_to_all(outgoing, 'tile', split_axis=0, concat_axis=0, tiled=True)  50 us
    convert_element_type x2, local copies, waits for them, and re-layouts, shards(): rotated.astype(jnp.float32)  31.5 us
    all_gather x1, blocking collectives, shards(): all_refs = lax.all_gather(own_refs, 'cls', axis=0, tiled=True)  25.5 us
    all_to_all x3, local copies, waits for them, and re-layouts, shards(): lax.all_to_all(outgoing, 'tile', split_axis=0, concat_axis=0, tiled=True)  22.3 us
    convert_element_type x1, local copies, waits for them, and re-layouts, unrotate(): back_two = jnp.einsum('orlab,obj->orjla', back_one, interp[:, 1], preferr...  19.8 us
    convert_element_type x1, local copies, waits for them, and re-layouts, rotate(): second_pass = jnp.einsum('orcij,obj->orbci', first_pass, interp[:, 1], pr...  16.8 us
  transfers between devices with their start and end apart: 5, of which 3 were waited for; matrix products, arithmetic and copies ran while one was open for 20% of the time, Pallas kernels for 0%

commit v1 on v0

v1 whole, which is shorter than its diff:
```python
import math

import jax
import jax.numpy as jnp
from jax import lax
from jax.sharding import PartitionSpec as P

F32 = jnp.float32
BF = jnp.bfloat16


def shards(subvols, tomogram, sharpness, references, interp, weighting):
    count, voxels = subvols.shape
    orients, edge = interp.shape[0], interp.shape[-1]
    refs = lax.all_gather(references, "cls", axis=0, tiled=True)
    weight = lax.all_gather(weighting, "tile", axis=0, tiled=True)
    number = refs.shape[0]
    plane = edge * edge
    kron = jnp.einsum("obj,ocl->obcjl", interp[:, 1].astype(F32), interp[:, 2].astype(F32))
    kron = kron.astype(BF).reshape(orients, plane, plane)
    second = jnp.einsum(
        "rip,oqp->oriq", refs.reshape(number, edge, plane), kron, preferred_element_type=F32
    ).astype(BF)
    rotated = jnp.einsum("oriq,oai->oraq", second, interp[:, 0], preferred_element_type=F32)
    rotated = rotated.astype(BF).reshape(orients, number, voxels)
    own = jnp.take(weight, tomogram[:, 0], axis=0)
    weighted = (subvols.astype(F32)[:, None, :] * own.astype(F32)).astype(BF)
    scores = jnp.einsum("sov,orv->sor", weighted, rotated, preferred_element_type=F32)
    scores = scores * (sharpness.astype(F32) / math.sqrt(voxels))[:, None, None]
    weights = jax.nn.softmax(scores.reshape(count, -1), axis=1).reshape(scores.shape)
    posterior = jnp.sum(weights, axis=1)
    acc = jnp.einsum("sor,sov->orv", weights.astype(BF), weighted, preferred_element_type=F32)
    acc = acc.astype(BF).reshape(orients, number, edge, plane)
    back = jnp.einsum("oraq,oai->oriq", acc, interp[:, 0], preferred_element_type=F32).astype(BF)
    summed = jnp.einsum("oriq,oqp->rip", back, kron, preferred_element_type=F32)
    summed = summed.reshape(number, voxels).astype(BF)
    own_sum = lax.psum_scatter(summed, "cls", scatter_dimension=0, tiled=True)
    own_sum = lax.psum(own_sum, "tile").astype(F32)
    spread = jnp.sqrt(jnp.mean(own_sum * own_sum, axis=1, keepdims=True) + 1e-06)
    return (own_sum / spread).astype(BF), posterior


def solution(mesh):
    in_specs = (
        P(("tile", "cls"), None),
        P(("tile", "cls"), None),
        P(("tile", "cls")),
        P("cls", None),
        P(),
        P("tile", None, None),
    )
    out_specs = (P("cls", None), P(("tile", "cls"), None))
    return jax.shard_map(shards, mesh=mesh, in_specs=in_specs, out_specs=out_specs, check_vma=False)
```

time: 480 us -> 355 us (0.74); the launches traced: 474 us -> 354 us
  local copies, waits for them, and re-layouts: 123 us -> 66.3 us
  waiting for transfers between devices: 221 us -> 188 us
  starting transfers between devices: 28.6 us -> 0.12 us
  matrix products: 51.2 us -> 37.5 us
  other arithmetic: 9.09 us -> 21.6 us
    convert_element_type x4 -> x0, local copies, waits for them, and re-layouts: 68.1 us -> none  [the longest x2 31.5 us: shards(): rotated.astype(jnp.float32)]
    all_to_all x3 -> x0, waiting for transfers between devices: 50 us -> none  [the longest x1 50 us: shards(): lax.all_to_all(outgoing, 'tile', split_axis=0, concat_axis=0, tiled=True)]
    reshape x2, local copies, waits for them, and re-layouts: 9.59 us -> 49.6 us  [the longest x1 45.3 us: shards(): kron = kron.astype(BF).reshape(orients, plane, plane)]
    all_to_all x3 -> x0, starting transfers between devices: 28.5 us -> none  [the longest x1 12.9 us: shards(): lax.all_to_all(outgoing, 'tile', split_axis=0, concat_axis=0, tiled=True)]
    all_to_all x4 -> x0, local copies, waits for them, and re-layouts: 23 us -> none  [the longest x3 22.3 us: shards(): lax.all_to_all(outgoing, 'tile', split_axis=0, concat_axis=0, tiled=True)]
    unnamed x3 -> x4, waiting for transfers between devices: 58.1 us -> 74 us
    dot_general x7 -> x4, matrix products: 51.2 us -> 37.5 us  [the longest x1 11.1 us: shards(): jnp.einsum('sor,sov->orv', weights.astype(BF), weighted, preferred_elemen...]
    convert_element_type x3, other arithmetic: 2.49 us -> 15.2 us  [the longest x1 11.3 us: shards(): kron = kron.astype(BF).reshape(orients, plane, plane)]
  transfers between devices with their start and end apart: 5 -> 3, of which waited for: 3 -> 2; matrix products, arithmetic and copies ran while one was open for 20% -> 22% of each run, Pallas kernels for 0% -> 0%
where the time goes in v1:
time: 355 us; the launch traced here: 354 us
  waiting for transfers between devices  188 us (53%)
  local copies, waits for them, and re-layouts  66.3 us (19%)
  matrix products  37.5 us (11%)
  blocking collectives  25.8 us (7%)
  other arithmetic  21.6 us (6%)
  between operations  14.5 us (4%)
    psum x1, waiting for transfers between devices, shards(): own_sum = lax.psum(own_sum, 'tile').astype(F32)  114 us
    unnamed x4, waiting for transfers between devices  74 us
    reshape x1, local copies, waits for them, and re-layouts, shards(): kron = kron.astype(BF).reshape(orients, plane, plane)  45.3 us
    all_gather x1, blocking collectives, shards(): refs = lax.all_gather(references, 'cls', axis=0, tiled=True)  25.8 us
    gather x1, local copies, waits for them, and re-layouts, shards(): own = jnp.take(weight, tomogram[:, 0], axis=0)  12.5 us
    convert_element_type x1, other arithmetic, shards(): kron = kron.astype(BF).reshape(orients, plane, plane)  11.3 us
    dot_general x1, matrix products, shards(): jnp.einsum('sor,sov->orv', weights.astype(BF), weighted, preferred_elemen...  11.1 us
    dot_general x1, matrix products, shards(): jnp.einsum('sov,orv->sor', weighted, rotated, preferred_element_type=F32)  10.7 us
  transfers between devices with their start and end apart: 3, of which 2 were waited for; matrix products, arithmetic and copies ran while one was open for 22% of the time, Pallas kernels for 0%

profile of v1, /device:TPU:1, one launch (start us, length us, event | category | flops | bytes accessed | tf_op | source)
XLA Modules:
  0.0 353.7 jit_solution(17544355098301408270)
XLA Ops:
  7.2 0.0 all-gather.3.cloned.1.call-start
  7.2 0.7 all-gather.3.cloned.1.call-update
  7.9 0.0 all-reduce.6.cloned.1.call-start
  7.9 0.8 bitcast_convert_fusion.1
  8.7 11.3 %fusion = bf16[4,32,32,32,32]{4,3,2,1,0:T(8,128)(2,1)} fusion(f32[4,32,32]{2,1,0:T(8,128)S(1)} %get-tuple-element.3, f32[4,32,32]{2,1,0:T(8,128)S(1)} %get-tuple-element.2), kind=kLoop, calls=%fused_computation.3 | loop fusion | flops 8388608 | bytes 8421376 | tf_op jit(solution)/shard_map/convert_element_type | solution.py:20
  20.0 45.3 %reshape.79 = bf16[4,1024,1024,1]{2,1,0,3:T(8,128)(2,1)} reshape(bf16[4,32,32,32,32]{4,3,2,1,0:T(8,128)(2,1)} %fusion) | data formatting | bytes 16777216 | tf_op jit(solution)/shard_map/reshape | solution.py:20
  65.4 25.8 %all-gather = bf16[8,1,32768]{2,1,0:T(2,128)(2,1)S(1)} all-gather(bf16[1,1,32768]{2,1,0:T(2,128)(2,1)S(1)} %bitcast.84), channel_id=1, replica_groups=mesh['tile'=32,'cls'=8] {'cls'}, dimensions={0}, use_global_device_ids=true | all-gather | bytes 589824 | tf_op jit(solution)/shard_map/all_gather | solution.py:15
  91.2 3.2 reduce.5
  94.3 8.0 %convert_bitcast_fusion = bf16[4,8,32,1024]{3,2,1,0:T(8,128)(2,1)} fusion(bf16[4,1024,1024,1]{2,1,0,3:T(8,128)(2,1)} %reshape.79, bf16[1,8,32,1024]{3,1,2,0:T(8,128)(2,1)S(1)} %bitcast.83, bf16[4,3,32,32]{3,2,1,0:T(8,128)(2,1)S(1)} %copy-done.4), kind=kOutput, calls=%fused_computation.15 | convolution fusion | flops 2216689664 | bytes 11042816 | tf_op jit(solution)/shard_map/oriq,oai->oraq/dot_general | solution.py:24
  102.4 4.2 %reshape.64 = bf16[4,8,32768]{2,1,0:T(8,128)(2,1)} reshape(bf16[4,8,32,1024]{3,2,1,0:T(8,128)(2,1)} %convert_bitcast_fusion) | data formatting | bytes 4194304 | tf_op jit(solution)/shard_map/reshape | solution.py:25
  106.6 2.2 convert_element_type.62
  109.0 12.5 %gather_fusion = bf16[32,4,32768]{2,1,0:T(4,128)(2,1)} fusion(bf16[32,4,32768]{2,1,0:T(4,128)(2,1)} %all-gather.3.cloned.1.call-done, s32[1024]{0:T(1024)S(1)} %pad_clamp_fusion), kind=kCustom, calls=%fused_computation | custom fusion | bytes 16777344 | tf_op jit(solution)/shard_map/jit(_take)/gather | solution.py:26
  121.5 10.7 %fusion.52 = (f32[32]{0:T(128)S(1)}, f32[4,8,32]{2,1,0:T(8,128)S(1)}) fusion(f32[32]{0:T(128)S(1)} %convert_multiply_fusion, bf16[4,8,32768]{2,1,0:T(8,128)(2,1)} %reshape.64, bf16[32,4,32768]{2,1,0:T(4,128)(2,1)} %gather_fusion, f32[32,32768]{1,0:T(8,128)} %convert_element_type.62, pred[32]{0:T(512)(128)(4,1)S(1)} %and_bitcast_fusion), kind=kOutput, calls=%fused_computation.42 | convolution fusion | flops 83888096 | bytes 14684448 | tf_op jit(solution)/shard_map/sov,orv->sor/dot_general | solution.py:28
  132.3 11.1 %convolution_convert_fusion = bf16[4,8,32768]{2,1,0:T(8,128)(2,1)} fusion(f32[4,8,32]{2,1,0:T(8,128)S(1)} %get-tuple-element.5, f32[32]{0:T(128)S(1)} %fusion.49, f32[32]{0:T(128)S(1)} %get-tuple-element.4, bf16[32,4,32768]{2,1,0:T(4,128)(2,1)S(1)} %copy-done.1, f32[32,32768]{1,0:T(8,128)S(1)} %copy-done, pred[32]{0:T(512)(128)(4,1)S(1)} %and_bitcast_fusion), kind=kOutput, calls=%fused_computation.2 | convolution fusion | flops 84937728 | bytes 14684448 | tf_op jit(solution)/shard_map/sor,sov->orv/dot_general | solution.py:32
  143.3 7.6 %fusion.33 = bf16[1,8,32,1024]{3,2,1,0:T(8,128)(2,1)S(1)} fusion(bf16[4,1024,1024,1]{2,1,0,3:T(8,128)(2,1)} %reshape.79, bf16[4,8,32,1024]{3,1,2,0:T(8,128)(2,1)} %bitcast.82, bf16[4,3,32,32]{3,2,1,0:T(8,128)(2,1)S(1)} %copy-done.4), kind=kOutput, calls=%fused_computation.19 | convolution fusion | flops 2215903232 | bytes 11042816 | tf_op jit(solution)/shard_map/oriq,oqp->rip/dot_general | solution.py:35
  151.0 1.1 copy.33
  152.1 0.0 all-reduce.4.cloned.1.call-start
  152.2 0.6 dynamic-slice
  152.8 73.3 %all-reduce.6.cloned.1.call-done = bf16[8,32768]{1,0:T(8,128)(2,1)} async-done(((bf16[8,32768]{1,0:T(8,128)(2,1)}), bf16[8,32768]{1,0:T(8,128)(2,1)}) %all-reduce.6.cloned.1.call-update) | async-done | bytes 524304
  226.1 2.5 constant_dynamic-slice_fusion
  228.6 0.6 bitcast_reduce_fusion
  229.2 113.8 %all-reduce.4.cloned.1.call-done = bf16[1,32768]{1,0:T(2,128)(2,1)} async-done(((bf16[1,32768]{1,0:T(2,128)(2,1)}), bf16[1,32768]{1,0:T(2,128)(2,1)}) %all-reduce.4.cloned.1.call-update) | async-done | bytes 65552 | tf_op jit(solution)/shard_map/psum | solution.py:38
  343.0 1.8 multiply_reduce_fusion
  345.5 1.7 divide_convert_fusion
  (24 shorter events, 0.1 us)
Async XLA Ops:
  7.2 101.8 %all-gather.3.cloned.1.call-start = ((), (), s32[]{:S(2)}) async-start(), calls=%async_computation | async-start | bytes 8650752 | tf_op jit(solution)/shard_map/all_gather | solution.py:16
  7.9 218.2 %all-reduce.6.cloned.1.call-start = ((), (), s32[]{:S(2)}) async-start(), calls=%async_computation.2 | async-start | bytes 1048576
  20.0 45.3 %copy-start.3 = (bf16[1,32768]{1,0:T(2,128)(2,1)S(1)}, bf16[1,32768]{1,0:T(2,128)(2,1)}, u32[]{:S(2)}) copy-start(bf16[1,32768]{1,0:T(2,128)(2,1)} %param.9) | copy-start | bytes 196612
  20.0 74.3 %copy-start.4 = (bf16[4,3,32,32]{3,2,1,0:T(8,128)(2,1)S(1)}, bf16[4,3,32,32]{3,2,1,0:T(8,128)(2,1)}, u32[]{:S(2)}) copy-start(bf16[4,3,32,32]{3,2,1,0:T(8,128)(2,1)} %param.10) | copy-start | bytes 73732
  94.3 12.3 %copy-start.2 = (bf16[32,32768]{1,0:T(8,128)(2,1)S(1)}, bf16[32,32768]{1,0:T(8,128)(2,1)}, u32[]{:S(2)}) copy-start(bf16[32,32768]{1,0:T(8,128)(2,1)} %param.6) | copy-start | bytes 6291460
  102.4 6.5 %copy-start.5 = (s32[32,1]{0,1:T(1,128)S(1)}, s32[32,1]{0,1:T(1,128)}, u32[]{:S(2)}) copy-start(s32[32,1]{0,1:T(1,128)} %param.7) | copy-start | bytes 388
  102.4 6.5 %copy-start.6 = (bf16[32]{0:T(256)(128)(2,1)S(1)}, bf16[32]{0:T(256)(128)(2,1)}, u32[]{:S(2)}) copy-start(bf16[32]{0:T(256)(128)(2,1)} %param.8) | copy-start | bytes 196
  121.5 10.8 %copy-start = (f32[32,32768]{1,0:T(8,128)S(1)}, f32[32,32768]{1,0:T(8,128)}, u32[]{:S(2)}) copy-start(f32[32,32768]{1,0:T(8,128)} %convert_element_type.62) | copy-start | bytes 12582916
  121.5 10.8 %copy-start.1 = (bf16[32,4,32768]{2,1,0:T(4,128)(2,1)S(1)}, bf16[32,4,32768]{2,1,0:T(4,128)(2,1)}, u32[]{:S(2)}) copy-start(bf16[32,4,32768]{2,1,0:T(4,128)(2,1)} %gather_fusion) | copy-start | bytes 25165828
  143.3 8.8 %copy-start.7 = (u32[256]{0:T(256)S(1)}, u32[256]{0:T(256)}, u32[]{:S(2)}) copy-start(u32[256]{0:T(256)} %constant.38) | copy-start | bytes 3076
  152.1 190.9 %all-reduce.4.cloned.1.call-start = ((), (), s32[]{:S(2)}) async-start(), calls=%async_computation.1 | async-start | bytes 262144 | tf_op jit(solution)/shard_map/psum | solution.py:38
Sparse Core Ops, SparseCore 0:
  10.6 62.1 all-gather.2
  152.2 73.8 all-reduce.5
  230.2 112.7 all-reduce.3

commit v2 on v1

v2 whole, which is shorter than its diff:
```python
import functools
import math

import jax
import jax.numpy as jnp
from jax import lax
from jax.experimental import pallas as pl
from jax.experimental.pallas import tpu as pltpu
from jax.sharding import PartitionSpec as P

F32 = jnp.float32
BF = jnp.bfloat16
MESH = pl.DeviceIdType.MESH
EDGE = 32
PLANE = EDGE * EDGE
SIDE = 4
TILES = 32
DEPTH = 8
ORIENTS = 4
REFS = 8
ROWS = 32
CHUNKS = 8
PAIRS = CHUNKS // 2
NT = (((1,), (1,)), ((), ()))


def dot(a, b):
    return jnp.dot(a, b, preferred_element_type=F32)


def dot_nt(a, b):
    return lax.dot_general(a, b, NT, preferred_element_type=F32)


def iota(shape, dim):
    return lax.broadcasted_iota(jnp.int32, shape, dim)


def mask(cond):
    return jnp.where(cond, 1.0, 0.0).astype(BF)


def kernel(
    x_ref, tom_ref, sharp_ref, own_ref, interp_ref, w_ref,
    upd_ref, post_ref,
    wall, kron, cur, second, rot, y, pick, rep, fwd, bwd, sc, acc, back, total,
    out_s, in_s, out_z, in_z, full,
    ws, wr, rs, rr, ps, pr, zs, zr, fs, fr,
):
    tile, z = lax.axis_index("tile"), lax.axis_index("cls")
    core, xx, yy = tile % 2, (tile // 2) % SIDE, tile // (2 * SIDE)

    def at(y_, x_, c_):
        return ((y_ * SIDE + x_) * 2 + c_, z)

    sibling = (tile + 1 - 2 * core, z)

    def peer(d):
        return ((tile + d) % TILES, z)

    def above(d):
        return (tile, (z + d) % DEPTH)

    def remote(src, dst, ssem, rsem, dev):
        return pltpu.make_async_remote_copy(
            src_ref=src, dst_ref=dst, send_sem=ssem, recv_sem=rsem, device_id=dev, device_id_type=MESH
        )

    wall[:, yy, xx, core] = w_ref[...]
    cur[z] = own_ref[...]

    barrier = pltpu.get_barrier_semaphore()

    @pl.loop(1, TILES)
    def _(d):
        pl.semaphore_signal(barrier, inc=1, device_id=peer(d), device_id_type=MESH)

    @pl.loop(1, DEPTH)
    def _(d):
        pl.semaphore_signal(barrier, inc=1, device_id=above(d), device_id_type=MESH)

    pl.semaphore_wait(barrier, TILES - 1 + DEPTH - 1)

    half = pl.ds(pl.multiple_of(core * 16, 16), 16)

    def ref_copy(d):
        return remote(cur.at[z, half], cur.at[z, half], rs.at[d], rr.at[d], above(d))

    def ref_swap():
        return remote(cur.at[:, half], cur.at[:, half], rs.at[0], rr.at[0], sibling)

    @pl.loop(1, DEPTH)
    def _(d):
        ref_copy(d).start()

    def step(ch, sign, xfirst, kind):
        if kind == 6:
            block = wall.at[ch, :, :, core]
            dev = sibling
        else:
            leg = kind // 3
            along_x = xfirst == (leg == 0)
            hop = (1, -1, sign)[kind % 3]
            fwd_from = 0 if kind % 3 < 2 else -hop
            px = (xx + fwd_from + SIDE) % SIDE if along_x else xx
            py = yy if along_x else (yy + fwd_from + SIDE) % SIDE
            dev = at(yy, (xx + hop + SIDE) % SIDE, core) if along_x else at((yy + hop + SIDE) % SIDE, xx, core)
            if leg == 0:
                block = wall.at[ch, py, px, core]
            elif along_x:
                block = wall.at[ch, :, px, core]
            else:
                block = wall.at[ch, py, :, core]
        return remote(block, block, ws.at[ch, kind], wr.at[ch, kind], dev)

    def go(j, kinds):
        for kind in kinds:
            step(2 * j, 1 - 2 * (j % 2), True, kind).start()
            step(2 * j + 1, 1 - 2 * (j % 2), False, kind).start()

    def landed(j, kinds):
        for kind in kinds:
            step(2 * j, 1 - 2 * (j % 2), True, kind).wait_recv()
            step(2 * j + 1, 1 - 2 * (j % 2), False, kind).wait_recv()

    for j in range(PAIRS):
        go(j, (0, 1))

    def comm(j):
        if 0 <= j < PAIRS:
            landed(j, (0, 1))
            go(j, (2,))
        if 0 <= j - 1 < PAIRS:
            landed(j - 1, (2,))
            go(j - 1, (3, 4))
        if 0 <= j - 2 < PAIRS:
            landed(j - 2, (3, 4))
            go(j - 2, (5,))
        if 0 <= j - 3 < PAIRS:
            landed(j - 3, (5,))
            go(j - 3, (6,))

    def build(o):
        a1 = dot(interp_ref[o, 1], mask(iota((EDGE, PLANE), 1) // EDGE == iota((EDGE, PLANE), 0)))
        a2 = dot(interp_ref[o, 2], mask(iota((EDGE, PLANE), 1) % EDGE == iota((EDGE, PLANE), 0)))
        rep[...] = a1

        @pl.loop(0, EDGE)
        def _(b):
            kron[o, pl.ds(pl.multiple_of(b * EDGE, EDGE), EDGE), :] = (rep[pl.ds(b, 1), :] * a2).astype(BF)

        a0 = interp_ref[o, 0]
        select = mask(iota((256, EDGE), 0) // REFS == iota((256, EDGE), 1))
        row, col = iota((256, 256), 0), iota((256, 256), 1)
        spread = mask(iota((EDGE, 256), 1) % EDGE == iota((EDGE, 256), 0))
        wide = dot(dot(select, a0).astype(BF), spread)
        fwd[o] = jnp.where(row % REFS == col // EDGE, wide, 0.0).astype(BF)
        spread = mask(iota((EDGE, 256), 1) // REFS == iota((EDGE, 256), 0))
        wide = dot(dot_nt(select, a0).astype(BF), spread)
        bwd[o] = jnp.where(row % REFS == col % REFS, wide, 0.0).astype(BF)

    def rotate(o):
        flat = cur[...].reshape(256, PLANE)

        @pl.loop(0, 4)
        def _(n):
            cols = pl.ds(pl.multiple_of(n * 256, 256), 256)
            part = dot_nt(flat, kron[o, cols, :]).astype(BF)
            rot[:, o, :, cols] = dot(fwd[o], part).reshape(EDGE, REFS, 256)

    def score(ch):
        @pl.loop(0, 4)
        def _(n):
            cols = pl.ds(pl.multiple_of(n * 256, 256), 256)
            got = dot(pick[...], wall[ch, :, :, :, :, cols].reshape(512, 256))
            for sub in range(4):
                start = pl.multiple_of((ch * 4 + sub) * PLANE + n * 256, 256)
                rows = x_ref[:, pl.ds(start, 256)].astype(F32)
                prod = got[sub * 128 : sub * 128 + 128].reshape(ORIENTS, ROWS, 256) * rows[None]
                y[ch * 4 + sub, :, cols] = prod.reshape(128, 256).astype(BF)

        @pl.loop(0, 4)
        def _(sub):
            a = ch * 4 + sub
            sc[...] += dot_nt(rot[a].reshape(32, PLANE).astype(BF), y[a])

    sc[...] = jnp.zeros_like(sc)
    for sub in range(4):
        for o in range(ORIENTS):
            code = tom_ref[...] * 16 + (o * 4 + sub)
            pick[pl.ds((sub * 4 + o) * ROWS, ROWS), :] = mask(code == iota((ROWS, 512), 1))

    build(0)
    comm(0)
    build(1)
    comm(1)
    build(2)
    build(3)

    @pl.loop(1, DEPTH)
    def _(d):
        ref_copy(d).wait_recv()

    ref_swap().start()
    comm(2)
    ref_swap().wait_recv()
    pl.loop(0, 2)(rotate)
    comm(3)
    pl.loop(2, 4)(rotate)
    for j in range(4, 8):
        comm(j)
        landed(j - 4, (6,))
        pl.loop(2 * (j - 4), 2 * (j - 4) + 2)(score)

    raw = sc[...]
    pair = iota((32, 128), 0) // REFS
    lane = iota((32, 128), 1) // ROWS
    raw = jnp.where(pair == lane, raw, 0.0)
    scores = raw[:, 0:32] + raw[:, 32:64] + raw[:, 64:96] + raw[:, 96:128]
    scores = scores * sharp_ref[...]
    top = jnp.max(scores, axis=0, keepdims=True)
    expo = jnp.exp(scores - top)
    weights = expo / jnp.sum(expo, axis=0, keepdims=True)
    post_ref[...] = weights[0:8] + weights[8:16] + weights[16:24] + weights[24:32]
    tiled = jnp.concatenate([weights] * 4, axis=1)
    mixed = jnp.where(pair == lane, tiled, 0.0).astype(BF)

    @pl.loop(0, EDGE)
    def _(a):
        acc[:, a] = dot(mixed, y[a]).reshape(ORIENTS, REFS, PLANE)

    @pl.loop(0, ORIENTS)
    def _(o):
        cols = pl.ds(pl.multiple_of(o * PLANE, PLANE), PLANE)
        back[:, cols] = dot(bwd[o], acc[o].reshape(256, PLANE).astype(BF)).astype(BF)

    @pl.loop(0, 4)
    def _(n):
        cols = pl.ds(pl.multiple_of(n * 256, 256), 256)
        total[:, cols] = dot(back[...], kron[:, :, cols].reshape(ORIENTS * PLANE, 256))

    @pl.loop(0, EDGE)
    def _(i):
        part = total[pl.ds(pl.multiple_of(i * REFS, REFS), REFS), :]
        out_s[i] = jnp.concatenate([part[:, :512], part[:, 512:]], axis=0).astype(BF)

    def part_copy(d):
        dev = peer(d)
        return remote(out_s.at[dev[0]], in_s.at[d], ps.at[d], pr.at[d], dev)

    @pl.loop(1, TILES)
    def _(d):
        part_copy(d).start()

    @pl.loop(1, TILES)
    def _(d):
        part_copy(d).wait_recv()

    mine = lax.fori_loop(1, TILES, lambda d, s: s + in_s[d].astype(F32), out_s[tile].astype(F32))
    for block in range(8):
        rows, cols = (block // 4) * 8, (block % 4) * 128
        out_z[:, block, :] = mine[rows : rows + 8, cols : cols + 128]

    def z_copy(d):
        dev = above(d)
        return remote(out_z.at[dev[1]], in_z.at[d], zs.at[d], zr.at[d], dev)

    @pl.loop(1, DEPTH)
    def _(d):
        z_copy(d).start()

    @pl.loop(1, DEPTH)
    def _(d):
        z_copy(d).wait_recv()

    full[tile] = lax.fori_loop(1, DEPTH, lambda d, s: s + in_z[d], out_z[z])

    def full_copy(d):
        return remote(full.at[tile], full.at[tile], fs.at[d], fr.at[d], peer(d))

    @pl.loop(1, TILES)
    def _(d):
        full_copy(d).start()

    @pl.loop(1, DEPTH)
    def _(d):
        ref_copy(d).wait_send()
        z_copy(d).wait_send()

    ref_swap().wait_send()
    for j in range(PAIRS):
        for kind in range(7):
            step(2 * j, 1 - 2 * (j % 2), True, kind).wait_send()
            step(2 * j + 1, 1 - 2 * (j % 2), False, kind).wait_send()

    @pl.loop(1, TILES)
    def _(d):
        part_copy(d).wait_send()

    @pl.loop(1, TILES)
    def _(d):
        full_copy(d).wait_recv()

    whole = full[...].reshape(256, 128)
    mean = jnp.sum(whole * whole) / (EDGE * PLANE)
    upd_ref[...] = (whole / jnp.sqrt(mean + 1e-06)).astype(BF)

    @pl.loop(1, TILES)
    def _(d):
        full_copy(d).wait_send()


def shards(subvols, tomogram, sharpness, references, interp, weighting):
    rows, voxels = subvols.shape
    sharp = (sharpness.astype(F32) / math.sqrt(voxels)).reshape(1, rows)
    own = references.reshape(EDGE, PLANE)
    weight = weighting.reshape(ORIENTS, CHUNKS, 4, PLANE).transpose(1, 0, 2, 3).reshape(CHUNKS, 16, PLANE)
    vmem = pl.BlockSpec(memory_space=pltpu.VMEM)
    dma = pltpu.SemaphoreType.DMA
    updated, posterior = pl.pallas_call(
        kernel,
        out_shape=(
            jax.ShapeDtypeStruct((256, 128), BF),
            jax.ShapeDtypeStruct((REFS, rows), F32),
        ),
        in_specs=[vmem] * 6,
        out_specs=(vmem, vmem),
        scratch_shapes=[
            pltpu.VMEM((CHUNKS, SIDE, SIDE, 2, 16, PLANE), BF),
            pltpu.VMEM((ORIENTS, PLANE, PLANE), BF),
            pltpu.VMEM((REFS, EDGE, PLANE), BF),
            pltpu.VMEM((256, PLANE), BF),
            pltpu.VMEM((EDGE, ORIENTS, REFS, PLANE), F32),
            pltpu.VMEM((EDGE, ORIENTS * rows, PLANE), BF),
            pltpu.VMEM((512, 512), BF),
            pltpu.VMEM((EDGE, PLANE), F32),
            pltpu.VMEM((ORIENTS, 256, 256), BF),
            pltpu.VMEM((ORIENTS, 256, 256), BF),
            pltpu.VMEM((32, 128), F32),
            pltpu.VMEM((ORIENTS, EDGE, REFS, PLANE), F32),
            pltpu.VMEM((256, ORIENTS * PLANE), BF),
            pltpu.VMEM((256, PLANE), F32),
            pltpu.VMEM((TILES, 16, 512), BF),
            pltpu.VMEM((TILES, 16, 512), BF),
            pltpu.VMEM((REFS, 8, 128), F32),
            pltpu.VMEM((DEPTH, 8, 128), F32),
            pltpu.VMEM((TILES, 8, 128), F32),
            dma((CHUNKS, 7)),
            dma((CHUNKS, 7)),
            dma((DEPTH,)),
            dma((DEPTH,)),
            dma((TILES,)),
            dma((TILES,)),
            dma((DEPTH,)),
            dma((DEPTH,)),
            dma((TILES,)),
            dma((TILES,)),
        ],
        compiler_params=pltpu.CompilerParams(
            collective_id=0, has_side_effects=True, vmem_limit_bytes=56 * 1024 * 1024
        ),
    )(subvols, tomogram, sharp, own, interp, weight)
    return updated.reshape(1, voxels), posterior.T


def solution(mesh):
    in_specs = (
        P(("tile", "cls"), None),
        P(("tile", "cls"), None),
        P(("tile", "cls")),
        P("cls", None),
        P(),
        P("tile", None, None),
    )
    out_specs = (P("cls", None), P(("tile", "cls"), None))
    return jax.shard_map(shards, mesh=mesh, in_specs=in_specs, out_specs=out_specs, check_vma=False)
```

time: 355 us -> 95.2 us (0.27)
  waiting for transfers between devices: 188 us -> 0 us
  Pallas kernels: 0 us -> 84.9 us
  local copies, waits for them, and re-layouts: 66.3 us -> 6.87 us
  matrix products: 37.5 us -> 0 us
  blocking collectives: 25.8 us -> 0 us
  other arithmetic: 21.6 us -> 2.43 us
  between operations: 14.5 us -> 0.66 us
    psum x1 -> x0, waiting for transfers between devices: 114 us -> none  [shards(): own_sum = lax.psum(own_sum, 'tile').astype(F32)]
    pallas_call x0 -> x1, Pallas kernels: none -> 84.9 us  [shards(): pl.pallas_call(kernel, out_shape=(jax.ShapeDtypeStruct((256, 128), BF), j...]
    unnamed x4 -> x0, waiting for transfers between devices: 74 us -> none
    reshape x2 -> x4, local copies, waits for them, and re-layouts: 49.6 us -> 2.67 us  [the longest x3 2.01 us: shards(): weighting.reshape(ORIENTS, CHUNKS, 4, PLANE).transpose(1, 0, 2, 3)]
    dot_general x4 -> x0, matrix products: 37.5 us -> none  [the longest x1 11.1 us: shards(): jnp.einsum('sor,sov->orv', weights.astype(BF), weighted, preferred_elemen...]
    all_gather x1 -> x0, blocking collectives: 25.8 us -> none  [shards(): refs = lax.all_gather(references, 'cls', axis=0, tiled=True)]
    convert_element_type x3 -> x0, other arithmetic: 15.2 us -> none  [the longest x1 11.3 us: shards(): kron = kron.astype(BF).reshape(orients, plane, plane)]
    gather x1 -> x0, local copies, waits for them, and re-layouts: 12.5 us -> none  [shards(): own = jnp.take(weight, tomogram[:, 0], axis=0)]
  transfers between devices with their start and end apart: 3 -> 0, of which waited for: 2 -> 0; matrix products, arithmetic and copies ran while one was open for 22% -> 0% of each run, Pallas kernels for 0% -> 0%
where the time goes in v2:
time: 95.2 us; the launch traced here: 94.9 us
  Pallas kernels  84.9 us (89%)
  local copies, waits for them, and re-layouts  6.87 us (7%)
  other arithmetic  2.43 us (3%)
    pallas_call x1, Pallas kernels, shards(): pl.pallas_call(kernel, out_shape=(jax.ShapeDtypeStruct((256, 128), BF), j...  84.9 us
    unnamed x3, local copies, waits for them, and re-layouts  4.2 us
    reshape x3, local copies, waits for them, and re-layouts, shards(): weighting.reshape(ORIENTS, CHUNKS, 4, PLANE).transpose(1, 0, 2, 3)  2.01 us

profile of v2, /device:TPU:1, one launch (start us, length us, event | category | flops | bytes accessed | tf_op | source)
XLA Modules:
  0.0 94.9 jit_solution(1041900340875927813)
XLA Ops:
  0.6 1.2 %reshape.21 = bf16[4,8,4,1024]{3,2,1,0:T(4,128)(2,1)S(1)} reshape(bf16[1,4,32768]{2,1,0:T(4,128)(2,1)} %param.11) | data formatting | bytes 524288 | tf_op jit(solution)/shard_map/reshape | solution.py:317
  1.8 0.1 copy.13
  1.9 0.8 reshape.22.w_ref
  2.7 1.3 %reduce = bf16[32768]{0:T(1024)(128)(2,1)S(1)} reduce(bf16[1,32768]{1,0:T(2,128)(2,1)} %param.9, bf16[]{:T(256)} %constant.8), dimensions={0}, to_apply=%param.9.reduce_sub_computation | reduce | bytes 131074 | tf_op args[3]
  3.9 0.7 reshape.20.own_ref
  4.6 1.3 %copy.9.tom_ref = s32[32,1]{1,0:T(8,128)} copy(s32[32,1]{0,1:T(1,128)} %param.7) | data formatting | bytes 256 | tf_op args[1]
  5.9 1.2 %multiply_bitcast_fusion.sharp_ref = f32[1,32]{1,0:T(1,128)} fusion(bf16[32]{0:T(256)(128)(2,1)} %param.8), kind=kLoop, calls=%fused_computation.2 | loop fusion | flops 64 | bytes 192 | tf_op jit(solution)/shard_map/reshape | solution.py:315
  7.1 84.9 %shard_map.77 = (bf16[256,128]{1,0:T(8,128)(2,1)}, f32[8,32]{1,0:T(8,128)}) custom-call(bf16[32,32768]{1,0:T(8,128)(2,1)} %x_ref.1, s32[32,1]{1,0:T(8,128)} %copy.9.tom_ref, f32[1,32]{1,0:T(1,128)} %multiply_bitcast_fusion.sharp_ref, bf16[32,1024]{1,0:T(8,128)(2,1)} %reshape.20.own_ref, bf16[4,3,32,32]{3,2,1,0:T(8,128)(2,1)} %interp_ref.1, ...), custom_call_target="tpu_custom_call" | custom-call | tf_op jit(solution)/shard_map/pallas_call | solution.py:320
  92.0 1.6 %copy.14 = bf16[1,1,256,128]{3,1,2,0:T(2,128)(2,1)} copy(bf16[1,1,256,128]{3,2,1,0:T(8,128)(2,1)} %bitcast.13) | data formatting | bytes 131072
  93.6 1.3 %copy.16 = f32[32,8]{0,1:T(8,128)} copy(f32[32,8]{0,1:T(8,128)} %bitcast.14) | data formatting | bytes 2048

commit v3 on v2

v3 whole, which is shorter than its diff:
```python
import functools
import math

import jax
import jax.numpy as jnp
from jax import lax
from jax.experimental import pallas as pl
from jax.experimental.pallas import tpu as pltpu
from jax.sharding import PartitionSpec as P

F32 = jnp.float32
BF = jnp.bfloat16
MESH = pl.DeviceIdType.MESH
EDGE = 32
PLANE = EDGE * EDGE
SIDE = 4
TILES = 32
DEPTH = 8
ORIENTS = 4
REFS = 8
ROWS = 32
CHUNKS = 8
PAIRS = 3
NT = (((1,), (1,)), ((), ()))


def dot(a, b):
    return jnp.dot(a, b, preferred_element_type=F32)


def dot_nt(a, b):
    return lax.dot_general(a, b, NT, preferred_element_type=F32)


def iota(shape, dim):
    return lax.broadcasted_iota(jnp.int32, shape, dim)


def mask(cond):
    return jnp.where(cond, 1.0, 0.0).astype(BF)


def kernel(
    x_hbm, tom_hbm, sharp_hbm, own_hbm, interp_hbm, w_hbm,
    upd_ref, post_ref,
    x_ref, tom_ref, sharp_ref, own_ref, interp_ref, w_ref,
    wall, kron, cur, stage, rot, y, pick, rep, fwd, bwd, sc, acc, back,
    out_s, near, both, in_s, out_z, in_z, full, flat,
    ls, ws, wr, rs, rr, qs, qr, ps, pr, zs, zr, fs, fr,
):
    places = (x_ref, tom_ref, sharp_ref, own_ref, interp_ref, w_ref)
    loads = [
        pltpu.make_async_copy(source, place, ls.at[n])
        for n, (source, place) in enumerate(zip((x_hbm, tom_hbm, sharp_hbm, own_hbm, interp_hbm, w_hbm), places))
    ]
    for n in (5, 3, 4, 1, 2, 0):
        loads[n].start()

    tile, z = lax.axis_index("tile"), lax.axis_index("cls")
    core, xx, yy = tile % 2, (tile // 2) % SIDE, tile // (2 * SIDE)

    def at(y_, x_, c_):
        return ((y_ * SIDE + x_) * 2 + c_, z)

    sibling = (tile + 1 - 2 * core, z)

    def peer(d):
        return ((tile + d) % TILES, z)

    def above(d):
        return (tile, (z + d) % DEPTH)

    def remote(src, dst, ssem, rsem, dev):
        return pltpu.make_async_remote_copy(
            src_ref=src, dst_ref=dst, send_sem=ssem, recv_sem=rsem, device_id=dev, device_id_type=MESH
        )

    barrier = pltpu.get_barrier_semaphore()

    @pl.loop(1, TILES)
    def _(d):
        pl.semaphore_signal(barrier, inc=1, device_id=peer(d), device_id_type=MESH)

    @pl.loop(1, DEPTH)
    def _(d):
        pl.semaphore_signal(barrier, inc=1, device_id=above(d), device_id_type=MESH)

    loads[3].wait()
    loads[5].wait()
    for a in range(EDGE):
        cols = slice(a * PLANE, (a + 1) * PLANE)
        stage[a // 4, (a % 4) * 4 : (a % 4) * 4 + 4, :] = w_ref[0, :, cols].astype(F32)
        rep[a : a + 1, :] = own_ref[:, cols].astype(F32)
    mine_first = pl.ds(2 - 2 * (z % 2), 2)
    wall[mine_first, 0, 0, core] = stage[mine_first].astype(BF)
    wall[4:, 0, 0, core] = stage[4:].astype(BF)
    half = pl.ds(pl.multiple_of(core * 16, 16), 16)
    cur[z, half] = rep[half, :].astype(BF)

    pl.semaphore_wait(barrier, TILES - 1 + DEPTH - 1)

    def ref_copy(d):
        return remote(cur.at[z, half], cur.at[z, half], rs.at[d], rr.at[d], above(d))

    def ref_swap():
        return remote(cur.at[:, half], cur.at[:, half], rs.at[0], rr.at[0], sibling)

    ours, theirs = 2 - 2 * (z % 2), 2 * (z % 2)
    HOPS, LANDS = (1, -1, 2), (3, 1, 2)

    def chunk(j, xfirst):
        start = (ours, 4, 6, theirs)[j]
        return start if xfirst else start + 1

    def step(j, xfirst, kind):
        ch = chunk(j, xfirst)

        def block(line, place):
            return wall.at[ch, line, place, core] if xfirst else wall.at[ch, place, line, core]

        def along(first, hop):
            if first == xfirst:
                return at(yy, (xx + hop + SIDE) % SIDE, core)
            return at((yy + hop + SIDE) % SIDE, xx, core)

        rest = pl.ds(1, 3)
        if kind < 3:
            source, target, dev = block(0, 0), block(0, LANDS[kind]), along(True, HOPS[kind])
        elif kind < 6:
            source, target, dev = block(0, 0), block(LANDS[kind - 3], 0), along(False, HOPS[kind - 3])
        elif kind == 8 and j < PAIRS - 1:
            sign = 1 - 2 * (j % 2)
            source, target, dev = block(2 + sign, rest), block(2, rest), along(False, sign)
        elif kind < 9:
            source, target, dev = block(0, rest), block(LANDS[kind - 6], rest), along(False, HOPS[kind - 6])
        else:
            source = target = block((0, 3, 1, 2)[(kind - 9) % 4], pl.ds(0, 4))
            dev = sibling if kind < 13 else above(1 if xfirst else DEPTH - 1)
        return remote(source, target, ws.at[ch, kind], wr.at[ch, kind], dev)

    def go(j, kinds):
        for kind in kinds:
            step(j, True, kind).start()
            step(j, False, kind).start()

    def landed(j, kinds):
        for kind in kinds:
            step(j, True, kind).wait_recv()
            step(j, False, kind).wait_recv()

    def second(j):
        landed(j, (0, 1, 2))
        go(j, ((13, 6, 7, 9), (6, 7, 9), (6, 7, 8, 9))[j])

    def third(j):
        landed(j, (3, 4, 6, 7))
        go(j, ((8, 14, 15, 10, 11), (8, 10, 11), (10, 11))[j])

    def fourth(j):
        landed(j, (5, 8))
        go(j, ((16, 12), (12,), (12,))[j])

    def beside(*lines):
        for line in lines:
            landed(3, (13 + line,))
            go(3, (9 + line,))

    def build(o):
        a1 = dot(interp_ref[o, 1], mask(iota((EDGE, PLANE), 1) // EDGE == iota((EDGE, PLANE), 0)))
        a2 = dot(interp_ref[o, 2], mask(iota((EDGE, PLANE), 1) % EDGE == iota((EDGE, PLANE), 0)))
        rep[...] = a1

        @pl.loop(0, EDGE)
        def _(b):
            kron[o, pl.ds(pl.multiple_of(b * EDGE, EDGE), EDGE), :] = (rep[pl.ds(b, 1), :] * a2).astype(BF)

        a0 = interp_ref[o, 0]
        select = mask(iota((256, EDGE), 0) // REFS == iota((256, EDGE), 1))
        row, col = iota((256, 256), 0), iota((256, 256), 1)
        spread = mask(iota((EDGE, 256), 1) % EDGE == iota((EDGE, 256), 0))
        wide = dot(dot(select, a0).astype(BF), spread)
        fwd[o] = jnp.where(row % REFS == col // EDGE, wide, 0.0).astype(BF)
        spread = mask(iota((EDGE, 256), 1) // REFS == iota((EDGE, 256), 0))
        wide = dot(dot_nt(select, a0).astype(BF), spread)
        bwd[o] = jnp.where(row % REFS == col % REFS, wide, 0.0).astype(BF)

    def rotate(o):
        volumes = cur[...].reshape(256, PLANE)
        for n in range(4):
            cols = slice(n * 256, (n + 1) * 256)
            part = dot_nt(volumes, kron[o, cols, :]).astype(BF)
            got = dot(fwd[o], part).reshape(CHUNKS, 4, REFS, 256)
            for sub in range(4):
                spot = slice(sub * PLANE + n * 256, sub * PLANE + (n + 1) * 256)
                rot[:, pl.ds(pl.multiple_of(o * REFS, REFS), REFS), spot] = got[:, sub]

    def weigh(ch):
        for h in range(2):
            for n in range(4):
                cols = slice(n * 256, (n + 1) * 256)
                got = dot(pick[...], wall[ch, :, :, :, h * 8 : h * 8 + 8, cols].reshape(256, 256))
                for sub in range(2):
                    spot = (h * 2 + sub) * PLANE + n * 256
                    rows = x_ref[:, pl.ds(pl.multiple_of(ch * 4 * PLANE + spot, 256), 256)].astype(F32)
                    prod = got[sub * 128 : sub * 128 + 128].reshape(ORIENTS, ROWS, 256) * rows[None]
                    y[ch, :, spot : spot + 256] = prod.reshape(128, 256).astype(BF)

    def fifth(j):
        landed(j, (9, 10, 11, 12))
        start = chunk(j, True)
        pl.loop(start, start + 2)(weigh)

    def score(ch):
        sc[...] += dot_nt(y[ch], rot[ch].astype(BF))

    go(0, (0, 1, 2, 3, 4, 5))
    go(1, (0, 1, 2))

    @pl.loop(1, DEPTH)
    def _(d):
        ref_copy(d).start()

    loads[4].wait()
    pl.loop(0, 2)(build)
    second(0)
    go(1, (3, 4, 5))
    go(2, (0, 1, 2))
    pl.loop(2, 4)(build)
    second(1)
    loads[1].wait()
    loads[2].wait()
    sc[...] = jnp.zeros_like(sc)
    diagonal = iota((ROWS, ROWS), 0) == iota((ROWS, ROWS), 1)
    named = jnp.sum(jnp.where(diagonal, tom_ref[...].astype(F32), 0.0), axis=1, keepdims=True).astype(jnp.int32)
    away_y = (named // (2 * SIDE) + SIDE - yy) % SIDE
    away_x = (named // 2 + SIDE - xx) % SIDE
    named = (away_y * SIDE + away_x) * 2 + named % 2
    for sub in range(2):
        for o in range(ORIENTS):
            code = named * 8 + (sub * 4 + o)
            pick[pl.ds((sub * 4 + o) * ROWS, ROWS), :] = mask(code == iota((ROWS, 256), 1))
    third(0)
    go(2, (3, 4, 5))
    second(2)

    @pl.loop(1, DEPTH)
    def _(d):
        ref_copy(d).wait_recv()

    ref_swap().start()
    fourth(0)
    third(1)
    ref_swap().wait_recv()
    pl.loop(0, 1)(rotate)
    third(2)
    fourth(1)
    beside(0)
    pl.loop(1, 2)(rotate)
    beside(1)
    fourth(2)
    pl.loop(2, 3)(rotate)
    beside(2, 3)
    loads[0].wait()
    fifth(0)
    pl.loop(3, 4)(rotate)
    fifth(1)
    fifth(2)
    pl.loop(4, 8)(score)
    fifth(3)
    pl.loop(0, 4)(score)

    raw = jnp.concatenate([sc[...], jnp.zeros((128, 96), F32)], axis=1).T[:32]
    pair = iota((32, 128), 0) // REFS
    lane = iota((32, 128), 1) // ROWS
    raw = jnp.where(pair == lane, raw, 0.0)
    scores = raw[:, 0:32] + raw[:, 32:64] + raw[:, 64:96] + raw[:, 96:128]
    scores = scores * (sharp_ref[...].astype(F32) * (1 / math.sqrt(EDGE * PLANE)))
    top = jnp.max(scores, axis=0, keepdims=True)
    expo = jnp.exp(scores - top)
    weights = expo / jnp.sum(expo, axis=0, keepdims=True)
    post_ref[...] = weights[0:8] + weights[8:16] + weights[16:24] + weights[24:32]
    tiled = jnp.concatenate([weights] * 4, axis=1)
    mixed = jnp.where(pair == lane, tiled, 0.0).astype(BF)

    @pl.loop(0, CHUNKS)
    def _(ch):
        got = dot(mixed, y[ch])
        for sub in range(4):
            acc[:, ch * 4 + sub] = got[:, sub * PLANE : (sub + 1) * PLANE].reshape(ORIENTS, REFS, PLANE)

    for o in range(ORIENTS):
        back[:, o * PLANE : (o + 1) * PLANE] = dot(bwd[o], acc[o].reshape(256, PLANE).astype(BF)).astype(BF)

    def owner(n, k):
        return (k * SIDE + (n + k) % SIDE) * 2 + core

    def pair_copy(n):
        return remote(out_s.at[n, 1 - core], near.at[n], qs.at[n], qr.at[n], sibling)

    def part_copy(n, k):
        chip = tile // 2
        return remote(both.at[n, k], in_s.at[chip], ps.at[n, k], pr.at[chip], (owner(n, k), z))

    def part_arrival(d):
        chip = (tile // 2 + d) % (TILES // 2)
        return remote(in_s.at[chip], in_s.at[chip], ps.at[0, 0], pr.at[chip], (tile, z))

    def send_parts(n):
        pair_copy(n).wait_recv()
        both[n] = (out_s[n, core].astype(F32) + near[n].astype(F32)).astype(BF)

        @pl.loop(0, SIDE)
        def _(k):
            @pl.when(owner(n, k) != tile)
            def _():
                part_copy(n, k).start()

    for n in range(4):
        got = dot(back[...], kron[:, :, n * 256 : (n + 1) * 256].reshape(ORIENTS * PLANE, 256)).astype(BF)
        for k in range(8):
            out_s[n, k % 2, k // 2] = got[k * 32 : k * 32 + 32]
        pair_copy(n).start()
        if n:
            send_parts(n - 1)
    send_parts(3)

    @pl.loop(1, TILES // 2)
    def _(d):
        part_arrival(d).wait_recv()

    def add(d, so_far):
        return so_far + in_s[(tile // 2 + d) % (TILES // 2)].astype(F32)

    mine = lax.fori_loop(1, TILES // 2, add, both[(xx - yy + SIDE) % SIDE, yy].astype(F32))
    for block in range(8):
        rows, cols = (block // 2) * 8, (block % 2) * 128
        out_z[:, block, :] = mine[rows : rows + 8, cols : cols + 128]

    def z_copy(d):
        dev = above(d)
        return remote(out_z.at[dev[1]], in_z.at[d], zs.at[d], zr.at[d], dev)

    @pl.loop(1, DEPTH)
    def _(d):
        z_copy(d).start()

    @pl.loop(1, DEPTH)
    def _(d):
        z_copy(d).wait_recv()

    full[tile] = lax.fori_loop(1, DEPTH, lambda d, s: s + in_z[d], out_z[z])

    def full_copy(d):
        return remote(full.at[tile], full.at[tile], fs.at[d], fr.at[d], peer(d))

    @pl.loop(1, TILES)
    def _(d):
        full_copy(d).start()

    @pl.loop(1, DEPTH)
    def _(d):
        z_copy(d).wait_send()

    ref_swap().wait_send()

    @pl.loop(1, DEPTH)
    def _(d):
        ref_copy(d).wait_send()

    for j in range(4):
        for kind in (range(17), range(13), range(13), range(9, 13))[j]:
            step(j, True, kind).wait_send()
            step(j, False, kind).wait_send()

    for n in range(4):
        pair_copy(n).wait_send()

        @pl.loop(0, SIDE)
        def _(k):
            @pl.when(owner(n, k) != tile)
            def _():
                part_copy(n, k).wait_send()

    @pl.loop(1, TILES)
    def _(d):
        full_copy(d).wait_recv()

    whole = full[...].reshape(256, 128)
    mean = jnp.sum(whole * whole) / (EDGE * PLANE)
    scale = 1 / jnp.sqrt(mean + 1e-06)
    for n in range(4):
        for k in range(8):
            got = full[(k // 2 * SIDE + (n + k // 2) % SIDE) * 2 + k % 2]
            for i in range(4):
                spot = (k * 4 + i) * 8 + n * 2
                flat[spot : spot + 2, :] = got[i * 2 : i * 2 + 2]
    upd_ref[...] = (flat[...] * scale).astype(BF)

    @pl.loop(1, TILES)
    def _(d):
        full_copy(d).wait_send()


def shards(subvols, tomogram, sharpness, references, interp, weighting):
    rows, voxels = subvols.shape
    vmem = pl.BlockSpec(memory_space=pltpu.VMEM)
    dma = pltpu.SemaphoreType.DMA
    updated, posterior = pl.pallas_call(
        kernel,
        out_shape=(
            jax.ShapeDtypeStruct((256, 128), BF),
            jax.ShapeDtypeStruct((REFS, rows), F32),
        ),
        in_specs=[pl.BlockSpec(memory_space=pl.ANY)] * 6,
        out_specs=(vmem, vmem),
        scratch_shapes=[
            pltpu.VMEM((rows, voxels), BF),
            pltpu.VMEM((1, rows), jnp.int32),
            pltpu.VMEM((1, rows), BF),
            pltpu.VMEM((1, voxels), BF),
            pltpu.VMEM((ORIENTS, 3, EDGE, EDGE), BF),
            pltpu.VMEM((1, ORIENTS, voxels), BF),
            pltpu.VMEM((CHUNKS, SIDE, SIDE, 2, 16, PLANE), BF),
            pltpu.VMEM((ORIENTS, PLANE, PLANE), BF),
            pltpu.VMEM((REFS, EDGE, PLANE), BF),
            pltpu.VMEM((CHUNKS, 16, PLANE), F32),
            pltpu.VMEM((CHUNKS, ORIENTS * REFS, 4 * PLANE), F32),
            pltpu.VMEM((CHUNKS, ORIENTS * rows, 4 * PLANE), BF),
            pltpu.VMEM((256, 256), BF),
            pltpu.VMEM((EDGE, PLANE), F32),
            pltpu.VMEM((ORIENTS, 256, 256), BF),
            pltpu.VMEM((ORIENTS, 256, 256), BF),
            pltpu.VMEM((128, 32), F32),
            pltpu.VMEM((ORIENTS, EDGE, REFS, PLANE), F32),
            pltpu.VMEM((256, ORIENTS * PLANE), BF),
            pltpu.VMEM((4, 2, SIDE, 32, 256), BF),
            pltpu.VMEM((4, SIDE, 32, 256), BF),
            pltpu.VMEM((4, SIDE, 32, 256), BF),
            pltpu.VMEM((TILES // 2, 32, 256), BF),
            pltpu.VMEM((REFS, 8, 128), F32),
            pltpu.VMEM((DEPTH, 8, 128), F32),
            pltpu.VMEM((TILES, 8, 128), F32),
            pltpu.VMEM((256, 128), F32),
            dma((6,)),
            dma((CHUNKS, 17)),
            dma((CHUNKS, 17)),
            dma((DEPTH,)),
            dma((DEPTH,)),
            dma((4,)),
            dma((4,)),
            dma((4, SIDE)),
            dma((TILES // 2,)),
            dma((DEPTH,)),
            dma((DEPTH,)),
            dma((TILES,)),
            dma((TILES,)),
        ],
        compiler_params=pltpu.CompilerParams(
            collective_id=0, has_side_effects=True, vmem_limit_bytes=56 * 1024 * 1024
        ),
    )(subvols, tomogram.reshape(1, rows), sharpness.reshape(1, rows), references, interp, weighting)
    return updated.reshape(1, voxels), posterior.T


def solution(mesh):
    in_specs = (
        P(("tile", "cls"), None),
        P(("tile", "cls"), None),
        P(("tile", "cls")),
        P("cls", None),
        P(),
        P("tile", None, None),
    )
    out_specs = (P("cls", None), P(("tile", "cls"), None))
    return jax.shard_map(shards, mesh=mesh, in_specs=in_specs, out_specs=out_specs, check_vma=False)
```

time: 95.2 us -> 78.1 us (0.82)
  Pallas kernels: 84.9 us -> 74.5 us
  local copies, waits for them, and re-layouts: 6.87 us -> 2.87 us
  other arithmetic: 2.43 us -> 0 us
    pallas_call x1, Pallas kernels: 84.9 us -> 74.5 us  [shards(): pl.pallas_call(kernel, out_shape=(jax.ShapeDtypeStruct((256, 128), BF), j...]
    reshape x4 -> x0, local copies, waits for them, and re-layouts: 2.67 us -> none  [the longest x3 2.01 us: shards(): weighting.reshape(ORIENTS, CHUNKS, 4, PLANE).transpose(1, 0, 2, 3)]
    unnamed x3 -> x2, local copies, waits for them, and re-layouts: 4.2 us -> 2.87 us
    unnamed x1 -> x0, other arithmetic: 1.26 us -> none
    reshape x1 -> x0, other arithmetic: 1.17 us -> none  [shards(): sharp = (sharpness.astype(F32) / math.sqrt(voxels)).reshape(1, rows)]
where the time goes in v3:
time: 78.1 us; the launch traced here: 78 us
  Pallas kernels  74.5 us (95%)
  local copies, waits for them, and re-layouts  2.87 us (4%)
    pallas_call x1, Pallas kernels, shards(): pl.pallas_call(kernel, out_shape=(jax.ShapeDtypeStruct((256, 128), BF), j...  74.5 us
    unnamed x2, local copies, waits for them, and re-layouts  2.87 us

profile of v3, /device:TPU:1, one launch (start us, length us, event | category | flops | bytes accessed | tf_op | source)
XLA Modules:
  0.0 78.0 jit_solution(12857517570691746206)
XLA Ops:
  0.6 74.5 %shard_map.77 = (bf16[256,128]{1,0:T(8,128)(2,1)}, f32[8,32]{1,0:T(8,128)}) custom-call(bf16[32,32768]{1,0:T(8,128)(2,1)} %x_hbm.1, s32[1,32]{1,0:T(1,128)} %bitcast.11, bf16[1,32]{1,0:T(2,128)(2,1)} %bitcast.12, bf16[1,32768]{1,0:T(2,128)(2,1)} %own_hbm.1, bf16[4,3,32,32]{3,2,1,0:T(8,128)(2,1)} %interp_hbm.1, bf16[1,4,32768]{2,1,0:T(4,128)(2,1)} %w_hbm.1), custom_call_target="tpu_custom_call" | custom-call | tf_op jit(solution)/shard_map/pallas_call | solution.py:408
  75.1 1.6 %copy.10 = bf16[1,1,256,128]{3,1,2,0:T(2,128)(2,1)} copy(bf16[1,1,256,128]{3,2,1,0:T(8,128)(2,1)} %bitcast.9) | data formatting | bytes 131072
  76.7 1.3 %copy.12 = f32[32,8]{0,1:T(8,128)} copy(f32[32,8]{0,1:T(8,128)} %bitcast.10) | data formatting | bytes 2048

commit v4 on v3

--- a/solution.py
+++ b/solution.py
@@ -205,11 +205,6 @@
                     prod = got[sub * 128 : sub * 128 + 128].reshape(ORIENTS, ROWS, 256) * rows[None]
                     y[ch, :, spot : spot + 256] = prod.reshape(128, 256).astype(BF)
 
-    def fifth(j):
-        landed(j, (9, 10, 11, 12))
-        start = chunk(j, True)
-        pl.loop(start, start + 2)(weigh)
-
     def score(ch):
         sc[...] += dot_nt(y[ch], rot[ch].astype(BF))
 
@@ -221,11 +216,17 @@
         ref_copy(d).start()
 
     loads[4].wait()
-    pl.loop(0, 2)(build)
-    second(0)
-    go(1, (3, 4, 5))
-    go(2, (0, 1, 2))
-    pl.loop(2, 4)(build)
+
+    @pl.loop(0, ORIENTS)
+    def _(o):
+        build(o)
+
+        @pl.when(o == 1)
+        def _():
+            second(0)
+            go(1, (3, 4, 5))
+            go(2, (0, 1, 2))
+
     second(1)
     loads[1].wait()
     loads[2].wait()
@@ -251,23 +252,40 @@
     fourth(0)
     third(1)
     ref_swap().wait_recv()
-    pl.loop(0, 1)(rotate)
-    third(2)
-    fourth(1)
-    beside(0)
-    pl.loop(1, 2)(rotate)
-    beside(1)
-    fourth(2)
-    pl.loop(2, 3)(rotate)
-    beside(2, 3)
+
+    @pl.loop(0, ORIENTS)
+    def _(o):
+        rotate(o)
+
+        @pl.when(o == 0)
+        def _():
+            third(2)
+            fourth(1)
+            beside(0)
+
+        @pl.when(o == 1)
+        def _():
+            beside(1)
+            fourth(2)
+
+        @pl.when(o == 2)
+        def _():
+            beside(2, 3)
+
     loads[0].wait()
-    fifth(0)
-    pl.loop(3, 4)(rotate)
-    fifth(1)
-    fifth(2)
-    pl.loop(4, 8)(score)
-    fifth(3)
-    pl.loop(0, 4)(score)
+
+    @pl.loop(0, 4)
+    def _(q):
+        for j in range(4):
+
+            @pl.when(q == j)
+            def _():
+                landed(j, (9, 10, 11, 12))
+
+        start = 2 + 2 * q - (q // 3) * 6
+        start = start + (1 - (q + 2) // 3) * (ours - 2) + (q // 3) * (theirs - 2)
+        pl.loop(start, start + 2)(weigh)
+        pl.loop(start, start + 2)(score)
 
     raw = jnp.concatenate([sc[...], jnp.zeros((128, 96), F32)], axis=1).T[:32]
     pair = iota((32, 128), 0) // REFS
@@ -288,8 +306,10 @@
         for sub in range(4):
             acc[:, ch * 4 + sub] = got[:, sub * PLANE : (sub + 1) * PLANE].reshape(ORIENTS, REFS, PLANE)
 
-    for o in range(ORIENTS):
-        back[:, o * PLANE : (o + 1) * PLANE] = dot(bwd[o], acc[o].reshape(256, PLANE).astype(BF)).astype(BF)
+    @pl.loop(0, ORIENTS)
+    def _(o):
+        cols = pl.ds(pl.multiple_of(o * PLANE, PLANE), PLANE)
+        back[:, cols] = dot(bwd[o], acc[o].reshape(256, PLANE).astype(BF)).astype(BF)
 
     def owner(n, k):
         return (k * SIDE + (n + k) % SIDE) * 2 + core
@@ -315,13 +335,18 @@
             def _():
                 part_copy(n, k).start()
 
-    for n in range(4):
-        got = dot(back[...], kron[:, :, n * 256 : (n + 1) * 256].reshape(ORIENTS * PLANE, 256)).astype(BF)
+    @pl.loop(0, 4)
+    def _(n):
+        cols = pl.ds(pl.multiple_of(n * 256, 256), 256)
+        got = dot(back[...], kron[:, :, cols].reshape(ORIENTS * PLANE, 256)).astype(BF)
         for k in range(8):
             out_s[n, k % 2, k // 2] = got[k * 32 : k * 32 + 32]
         pair_copy(n).start()
-        if n:
+
+        @pl.when(n > 0)
+        def _():
             send_parts(n - 1)
+
     send_parts(3)
 
     @pl.loop(1, TILES // 2)
@@ -372,7 +397,8 @@
             step(j, True, kind).wait_send()
             step(j, False, kind).wait_send()
 
-    for n in range(4):
+    @pl.loop(0, 4)
+    def _(n):
         pair_copy(n).wait_send()
 
         @pl.loop(0, SIDE)

time: 78.1 us -> 77 us (0.986)
  Pallas kernels: 74.5 us -> 73.4 us
    pallas_call x1, Pallas kernels: 74.5 us -> 73.4 us  [shards(): pl.pallas_call(kernel, out_shape=(jax.ShapeDtypeStruct((256, 128), BF), j...]
where the time goes in v4:
time: 77 us; the launch traced here: 76.9 us
  Pallas kernels  73.4 us (95%)
  local copies, waits for them, and re-layouts  2.87 us (4%)
    pallas_call x1, Pallas kernels, shards(): pl.pallas_call(kernel, out_shape=(jax.ShapeDtypeStruct((256, 128), BF), j...  73.4 us
    unnamed x2, local copies, waits for them, and re-layouts  2.87 us

profile of v4, /device:TPU:1, one launch (start us, length us, event | category | flops | bytes accessed | tf_op | source)
XLA Modules:
  0.0 76.9 jit_solution(16499378600669148005)
XLA Ops:
  0.6 73.4 %shard_map.77 = (bf16[256,128]{1,0:T(8,128)(2,1)}, f32[8,32]{1,0:T(8,128)}) custom-call(bf16[32,32768]{1,0:T(8,128)(2,1)} %x_hbm.1, s32[1,32]{1,0:T(1,128)} %bitcast.11, bf16[1,32]{1,0:T(2,128)(2,1)} %bitcast.12, bf16[1,32768]{1,0:T(2,128)(2,1)} %own_hbm.1, bf16[4,3,32,32]{3,2,1,0:T(8,128)(2,1)} %interp_hbm.1, bf16[1,4,32768]{2,1,0:T(4,128)(2,1)} %w_hbm.1), custom_call_target="tpu_custom_call" | custom-call | tf_op jit(solution)/shard_map/pallas_call | solution.py:434
  74.0 1.6 %copy.10 = bf16[1,1,256,128]{3,1,2,0:T(2,128)(2,1)} copy(bf16[1,1,256,128]{3,2,1,0:T(8,128)(2,1)} %bitcast.9) | data formatting | bytes 131072
  75.6 1.3 %copy.12 = f32[32,8]{0,1:T(8,128)} copy(f32[32,8]{0,1:T(8,128)} %bitcast.10) | data formatting | bytes 2048

commit v5 on v4

--- a/solution.py
+++ b/solution.py
@@ -249,8 +249,6 @@
         ref_copy(d).wait_recv()
 
     ref_swap().start()
-    fourth(0)
-    third(1)
     ref_swap().wait_recv()
 
     @pl.loop(0, ORIENTS)
@@ -259,31 +257,46 @@
 
         @pl.when(o == 0)
         def _():
+            fourth(0)
+
+        @pl.when(o == 1)
+        def _():
+            third(1)
+            beside(0)
+
+        @pl.when(o == 2)
+        def _():
             third(2)
+            beside(1)
+
+        @pl.when(o == 3)
+        def _():
             fourth(1)
-            beside(0)
-
-        @pl.when(o == 1)
-        def _():
-            beside(1)
-            fourth(2)
-
-        @pl.when(o == 2)
-        def _():
-            beside(2, 3)
+            beside(2)
 
     loads[0].wait()
 
     @pl.loop(0, 4)
     def _(q):
-        for j in range(4):
-
-            @pl.when(q == j)
-            def _():
-                landed(j, (9, 10, 11, 12))
-
-        start = 2 + 2 * q - (q // 3) * 6
-        start = start + (1 - (q + 2) // 3) * (ours - 2) + (q // 3) * (theirs - 2)
+        @pl.when(q == 0)
+        def _():
+            landed(0, (9, 10, 11, 12))
+
+        @pl.when(q == 1)
+        def _():
+            landed(1, (9, 10, 11, 12))
+            beside(3)
+
+        @pl.when(q == 2)
+        def _():
+            fourth(2)
+            landed(3, (9, 10, 11, 12))
+
+        @pl.when(q == 3)
+        def _():
+            landed(2, (9, 10, 11, 12))
+
+        start = (q % 2) * (3 + q) + (1 - q % 2) * (ours + (q // 2) * (theirs - ours))
         pl.loop(start, start + 2)(weigh)
         pl.loop(start, start + 2)(score)
 
@@ -349,11 +362,8 @@
 
     send_parts(3)
 
-    @pl.loop(1, TILES // 2)
-    def _(d):
+    def add(d, so_far):
         part_arrival(d).wait_recv()
-
-    def add(d, so_far):
         return so_far + in_s[(tile // 2 + d) % (TILES // 2)].astype(F32)
 
     mine = lax.fori_loop(1, TILES // 2, add, both[(xx - yy + SIDE) % SIDE, yy].astype(F32))

time: 77 us -> 73.3 us (0.952)
  Pallas kernels: 73.4 us -> 69.6 us
    pallas_call x1, Pallas kernels: 73.4 us -> 69.6 us  [shards(): pl.pallas_call(kernel, out_shape=(jax.ShapeDtypeStruct((256, 128), BF), j...]
where the time goes in v5:
time: 73.3 us; the launch traced here: 73.1 us
  Pallas kernels  69.6 us (95%)
  local copies, waits for them, and re-layouts  2.87 us (4%)
    pallas_call x1, Pallas kernels, shards(): pl.pallas_call(kernel, out_shape=(jax.ShapeDtypeStruct((256, 128), BF), j...  69.6 us
    unnamed x2, local copies, waits for them, and re-layouts  2.87 us

profile of v5, /device:TPU:1, one launch (start us, length us, event | category | flops | bytes accessed | tf_op | source)
XLA Modules:
  0.0 73.1 jit_solution(13349040436537639110)
XLA Ops:
  0.6 69.6 %shard_map.77 = (bf16[256,128]{1,0:T(8,128)(2,1)}, f32[8,32]{1,0:T(8,128)}) custom-call(bf16[32,32768]{1,0:T(8,128)(2,1)} %x_hbm.1, s32[1,32]{1,0:T(1,128)} %bitcast.11, bf16[1,32]{1,0:T(2,128)(2,1)} %bitcast.12, bf16[1,32768]{1,0:T(2,128)(2,1)} %own_hbm.1, bf16[4,3,32,32]{3,2,1,0:T(8,128)(2,1)} %interp_hbm.1, bf16[1,4,32768]{2,1,0:T(4,128)(2,1)} %w_hbm.1), custom_call_target="tpu_custom_call" | custom-call | tf_op jit(solution)/shard_map/pallas_call | solution.py:444
  70.2 1.6 %copy.10 = bf16[1,1,256,128]{3,1,2,0:T(2,128)(2,1)} copy(bf16[1,1,256,128]{3,2,1,0:T(8,128)(2,1)} %bitcast.9) | data formatting | bytes 131072
  71.8 1.3 %copy.12 = f32[32,8]{0,1:T(8,128)} copy(f32[32,8]{0,1:T(8,128)} %bitcast.10) | data formatting | bytes 2048

commit v6 on v5

--- a/solution.py
+++ b/solution.py
@@ -313,13 +313,13 @@
     tiled = jnp.concatenate([weights] * 4, axis=1)
     mixed = jnp.where(pair == lane, tiled, 0.0).astype(BF)
 
-    @pl.loop(0, CHUNKS)
+    @pl.loop(0, CHUNKS, unroll=4)
     def _(ch):
         got = dot(mixed, y[ch])
         for sub in range(4):
             acc[:, ch * 4 + sub] = got[:, sub * PLANE : (sub + 1) * PLANE].reshape(ORIENTS, REFS, PLANE)
 
-    @pl.loop(0, ORIENTS)
+    @pl.loop(0, ORIENTS, unroll=2)
     def _(o):
         cols = pl.ds(pl.multiple_of(o * PLANE, PLANE), PLANE)
         back[:, cols] = dot(bwd[o], acc[o].reshape(256, PLANE).astype(BF)).astype(BF)

time: 73.3 us -> 72.1 us (0.984)
  Pallas kernels: 69.6 us -> 68.4 us
    pallas_call x1, Pallas kernels: 69.6 us -> 68.4 us  [shards(): pl.pallas_call(kernel, out_shape=(jax.ShapeDtypeStruct((256, 128), BF), j...]
where the time goes in v6:
time: 72.1 us; the launch traced here: 71.9 us
  Pallas kernels  68.4 us (95%)
  local copies, waits for them, and re-layouts  2.87 us (4%)
    pallas_call x1, Pallas kernels, shards(): pl.pallas_call(kernel, out_shape=(jax.ShapeDtypeStruct((256, 128), BF), j...  68.4 us
    unnamed x2, local copies, waits for them, and re-layouts  2.87 us

profile of v6, /device:TPU:1, one launch (start us, length us, event | category | flops | bytes accessed | tf_op | source)
XLA Modules:
  0.0 71.9 jit_solution(15794512777632507186)
XLA Ops:
  0.6 68.4 %shard_map.77 = (bf16[256,128]{1,0:T(8,128)(2,1)}, f32[8,32]{1,0:T(8,128)}) custom-call(bf16[32,32768]{1,0:T(8,128)(2,1)} %x_hbm.1, s32[1,32]{1,0:T(1,128)} %bitcast.11, bf16[1,32]{1,0:T(2,128)(2,1)} %bitcast.12, bf16[1,32768]{1,0:T(2,128)(2,1)} %own_hbm.1, bf16[4,3,32,32]{3,2,1,0:T(8,128)(2,1)} %interp_hbm.1, bf16[1,4,32768]{2,1,0:T(4,128)(2,1)} %w_hbm.1), custom_call_target="tpu_custom_call" | custom-call | tf_op jit(solution)/shard_map/pallas_call | solution.py:444
  69.0 1.6 %copy.10 = bf16[1,1,256,128]{3,1,2,0:T(2,128)(2,1)} copy(bf16[1,1,256,128]{3,2,1,0:T(8,128)(2,1)} %bitcast.9) | data formatting | bytes 131072
  70.6 1.3 %copy.12 = f32[32,8]{0,1:T(8,128)} copy(f32[32,8]{0,1:T(8,128)} %bitcast.10) | data formatting | bytes 2048
